TPU v7x, 256 devices: a whole 4x4x8 slice. The times are simulated.
256 devices in a mesh: rows: 32 (over x, z_hi, core), feat: 8 (over y, z_lo).
Axes of the slice: x: 4, y: 4, z: 8 (z_hi: 4, z_lo: 2; z = z_hi * 2 + z_lo), core: 2. Of those that a mesh axis runs over, the one named last changes fastest.
Arguments:
- data: bfloat16 [196608, 1024], P(('rows', 'feat')), may hold values from -6 to 6
- rotation: bfloat16 [1024, 1024], P(None, 'feat'), may hold values from -0.1875 to 0.1875
- codebook: bfloat16 [256, 1024], P(None, 'feat'), may hold values from -5 to 5
Outputs:
- new_codebook: float32 [256, 1024], P(None, 'feat')
- counts: float32 [64, 256], P('feat')
- cross: float32 [1024, 1024], P('rows', 'feat')
All inputs are finite; a program needn't handle non-finite values.
Results may differ from a plain program's by a relative error of at most 0.0029.
Values may be sent and summed in bfloat16 or wider, within the bound.
No kernel may reach another device: no remote copies, remote signals or barrier semaphores. Data moves between devices by JAX's collectives and lax.ppermute only.
A program may use at most 64 MiB of HBM per device.

v0:
```python
import jax
import jax.numpy as jnp
from jax import lax
from jax.sharding import PartitionSpec as P

D = 1024
SUB = 64


inverse_temp = 0.5


def assign(grouped, code_local):
    rows_all, width = grouped.shape
    sub_width = D // SUB
    local_subs = width // sub_width
    words = code_local.shape[0]
    block = 1024
    codes = code_local.reshape(words, local_subs, sub_width)
    code_wide = code_local.astype(jnp.float32).reshape(words, local_subs, sub_width)
    squares = jnp.sum(code_wide * code_wide, axis=-1).T[:, None, :]

    def step(carry, piece):
        numer, counted = carry
        values = piece.reshape(block, local_subs, sub_width)
        dots = jnp.einsum("nsd,ksd->snk", values, codes, preferred_element_type=jnp.float32)
        logits = inverse_temp * (2.0 * dots - squares)
        weights = jax.nn.softmax(logits, axis=-1)
        weights_b = weights.astype(jnp.bfloat16)
        numer = numer + jnp.einsum(
            "snk,nsd->ksd", weights_b, values, preferred_element_type=jnp.float32
        ).reshape(words, width)
        counted = counted + jnp.sum(weights, axis=1)
        rebuilt = jnp.einsum("snk,ksd->nsd", weights_b, codes, preferred_element_type=jnp.float32)
        return ((numer, counted), rebuilt.reshape(block, width).astype(jnp.bfloat16))

    start = (jnp.zeros((words, width), jnp.float32), jnp.zeros((local_subs, words), jnp.float32))
    (numer, counted), rebuilt = lax.scan(
        step, start, grouped.reshape(rows_all // block, block, width)
    )
    return (numer, counted, rebuilt.reshape(rows_all, width))


def local(data, rotation, codebook):
    width = D
    full_rotation = lax.all_gather(rotation, "feat", axis=1, tiled=True)
    own = jnp.dot(data, full_rotation, preferred_element_type=jnp.float32).astype(jnp.bfloat16)
    grouped = lax.all_to_all(own, "feat", split_axis=1, concat_axis=0, tiled=True)
    numer, counted, rebuilt = assign(grouped, codebook)
    back = lax.all_to_all(rebuilt, "feat", split_axis=0, concat_axis=1, tiled=True)
    term = lax.dot_general(data, back, (((0,), (0,)), ((), ())), preferred_element_type=jnp.float32)
    n_rows = lax.axis_size("rows")
    n_feat = lax.axis_size("feat")
    ordered = term.reshape(n_rows, width // n_rows, n_feat, width // n_feat)
    ordered = ordered.transpose(0, 2, 1, 3).reshape(
        n_rows * n_feat * (width // n_rows), width // n_feat
    )
    cross = lax.psum_scatter(ordered, ("rows", "feat"), scatter_dimension=0, tiled=True)
    total_numer, total_counts = lax.psum((numer, counted), "rows")
    per_column = jnp.repeat(total_counts.T, D // SUB, axis=1)
    new_codebook = (total_numer + codebook.astype(jnp.float32)) / (per_column + 1.0)
    return (new_codebook, total_counts, cross)


def solution(mesh):
    in_specs = (P(("rows", "feat"), None), P(None, "feat"), P(None, "feat"))
    out_specs = (P(None, "feat"), P("feat", None), P("rows", "feat"))
    return jax.shard_map(local, mesh=mesh, in_specs=in_specs, out_specs=out_specs, check_vma=False)
```

profile of v0, /device:TPU:1, one launch (start us, length us, event | category | flops | bytes accessed | tf_op | source)
XLA Modules:
  0.0 1739.0 jit_solution(6497450159070339519)
XLA Ops:
  7.9 58.8 %all-gather.2.cloned.1.call-done = bf16[1024,1024]{1,0:T(8,128)(2,1)} async-done(((bf16[1024,128]{1,0:T(8,128)(2,1)}), bf16[1024,1024]{1,0:T(8,128)(2,1)}) %all-gather.2.cloned.1.call-update) | async-done | bytes 2097168 | tf_op jit(solution)/shard_map/all_gather | solution.py:46
  66.7 3.4 fusion.11
  70.1 1.4 copy.41
  71.5 4.3 all-to-all-start
  76.0 18.8 %all-to-all-done = bf16[768,8,128]{2,0,1:T(8,128)(2,1)} async-done(((bf16[768,8,128]{2,0,1:T(8,128)(2,1)}), bf16[768,8,128]{2,0,1:T(8,128)(2,1)}, u32[]{:S(2)}, u32[]{:S(2)}) %all-to-all-start) | async-done | bytes 1572896 | tf_op jit(solution)/shard_map/all_to_all | solution.py:48
  94.9 106.3 %while.15 = (s32[]{:T(128)}, f32[256,128]{0,1:T(8,128)S(1)}, f32[8,256]{1,0:T(8,128)S(1)}, bf16[6,1024,128]{2,1,0:T(8,128)(2,1)}, bf16[6,1024,128]{2,1,0:T(8,128...) while((s32[]{:T(128)}, f32[256,128]{0,1:T(8,128)S(1)}, ...), condition=%wide.region_5.6_spmd.clone, body=%wide.region_1.5_spmd.clone.sunk | while | flops 218302720 | bytes 49783428 | solution.py:38
  94.9 1.0 constant_dynamic-slice_fusion.2
  96.0 5.5 fusion.42
  101.5 4.2 fusion.43
  105.7 1.9 copy-done.1
  107.6 1.2 fusion.44
  108.8 2.8 convolution_convert_fusion.3
  112.6 1.0 constant_dynamic-slice_fusion.2
  113.7 5.5 fusion.42
  119.2 4.2 fusion.43
  123.4 1.9 copy-done.1
  125.3 1.2 fusion.44
  126.5 2.8 convolution_convert_fusion.3
  131.4 5.5 fusion.42
  136.9 4.2 fusion.43
  141.1 1.9 copy-done.1
  143.0 1.2 fusion.44
  144.2 2.8 convolution_convert_fusion.3
  149.1 5.5 fusion.42
  154.6 4.2 fusion.43
  158.8 1.9 copy-done.1
  160.7 1.2 fusion.44
  162.0 2.8 convolution_convert_fusion.3
  166.9 5.5 fusion.42
  172.4 4.2 fusion.43
  176.6 1.9 copy-done.1
  178.5 1.2 fusion.44
  179.7 2.8 convolution_convert_fusion.3
  184.6 5.5 fusion.42
  190.1 4.2 fusion.43
  194.3 1.9 copy-done.1
  196.2 1.2 fusion.44
  197.4 2.8 convolution_convert_fusion.3
  201.2 4.8 all-to-all-start.1
  206.8 18.3 %all-to-all-done.1 = bf16[8,768,128]{2,1,0:T(8,128)(2,1)S(1)} async-done(((bf16[8,768,128]{2,1,0:T(8,128)(2,1)}), bf16[8,768,128]{2,1,0:T(8,128)(2,1)S(1)}, u32[]{:S(2)}, u32[]{:S(2)}) %all-to-all-start.1) | async-done | bytes 1572896 | tf_op jit(solution)/shard_map/all_to_all | solution.py:50
  225.0 1.6 copy.29
  226.6 5.1 convolution_bitcast_fusion
  231.8 5.4 copy.30
  237.1 3.2 copy.39
  240.8 2.7 copy.31
  243.5 73.5 %psum.15 = f32[8,256]{1,0:T(8,128)S(1)} all-reduce(f32[8,256]{1,0:T(8,128)S(1)} %get-tuple-element.43), channel_id=1, replica_groups=mesh['rows'=32,'feat'=8] {'rows'}, use_global_device_ids=true, to_apply=%region_7.8 | all-reduce | flops 2048 | bytes 16384 | tf_op jit(solution)/shard_map/psum | solution.py:59
  317.0 154.0 %all-reduce.2.cloned.1.call-done = f32[256,128]{0,1:T(8,128)} async-done(((f32[256,128]{0,1:T(8,128)}), f32[256,128]{0,1:T(8,128)}) %all-reduce.2.cloned.1.call-update) | async-done | bytes 131088 | tf_op jit(solution)/shard_map/psum | solution.py:59
  472.7 1259.7 %reduce-scatter.2.cloned.1.call-done = f32[32,128]{1,0:T(8,128)} async-done(((f32[8192,128]{1,0:T(8,128)}), f32[32,128]{1,0:T(8,128)}) %reduce-scatter.2.cloned.1.call-update) | async-done | bytes 16400 | tf_op jit(solution)/shard_map/reduce_scatter | solution.py:58
  (63 shorter events, 14.3 us)
Async XLA Ops:
  7.2 59.5 %copy-start = (bf16[768,1024]{1,0:T(8,128)(2,1)S(1)}, bf16[768,1024]{1,0:T(8,128)(2,1)}, u32[]{:S(2)}) copy-start(bf16[768,1024]{1,0:T(8,128)(2,1)} %param.5) | copy-start | bytes 4718596
  7.2 59.5 %all-gather.2.cloned.1.call-start = ((), (), s32[]{:S(2)}) async-start(), calls=%async_computation.3 | async-start | bytes 2359296 | tf_op jit(solution)/shard_map/all_gather | solution.py:46
  70.1 5.8 copy-start.3
  71.5 23.3 %all-to-all-start = ((bf16[768,8,128]{2,0,1:T(8,128)(2,1)}), bf16[768,8,128]{2,0,1:T(8,128)(2,1)}, u32[]{:S(2)}, u32[]{:S(2)}) async-start(bf16[768,8,128]{2,0,1:T(8,128)(2,1)} %bitcast.50), calls=%async_computation | async-start | bytes 3145728 | tf_op jit(solution)/shard_map/all_to_all | solution.py:48
  105.6 1.9 copy-start.1
  123.4 1.9 copy-start.1
  141.1 1.9 copy-start.1
  158.8 1.9 copy-start.1
  176.5 1.9 copy-start.1
  194.3 1.9 copy-start.1
  201.2 4.8 copy-start.2
  201.2 23.9 %all-to-all-start.1 = ((bf16[8,768,128]{2,1,0:T(8,128)(2,1)}), bf16[8,768,128]{2,1,0:T(8,128)(2,1)S(1)}, u32[]{:S(2)}, u32[]{:S(2)}) async-start(bf16[8,768,128]{2,1,0:T(8,128)(2,1)} %bitcast.81), calls=%async_computation.1 | async-start | bytes 3145728 | tf_op jit(solution)/shard_map/all_to_all | solution.py:50
  206.0 265.1 %all-reduce.2.cloned.1.call-start = ((), (), s32[]{:S(2)}) async-start(), calls=%async_computation.4 | async-start | bytes 262144 | tf_op jit(solution)/shard_map/psum | solution.py:59
  206.7 1525.7 %reduce-scatter.2.cloned.1.call-start = ((), (), s32[]{:S(2)}) async-start(), calls=%async_computation.5 | async-start | bytes 4210688 | tf_op jit(solution)/shard_map/reduce_scatter | solution.py:58
  317.0 1415.4 %copy-start.4 = (f32[8,256]{1,0:T(8,128)}, f32[8,256]{1,0:T(8,128)S(1)}, u32[]{:S(2)}) copy-start(f32[8,256]{1,0:T(8,128)S(1)} %psum.15) | copy-start | bytes 24580
Sparse Core Ops, SparseCore 0:
  9.7 56.8 all-gather.1
  210.0 261.0 all-reduce.1
  474.3 1258.1 reduce-scatter.1
where the time goes:
time: 1750 us; the launch traced here: 1740 us
  waiting for transfers between devices  1510 us (86%)
  blocking collectives  73.5 us (4%)
  matrix products  65.5 us (4%)
  local copies, waits for them, and re-layouts  39.4 us (2%)
  other arithmetic  26.3 us (2%)
    reduce_scatter x1, waiting for transfers between devices, local(): lax.psum_scatter(ordered, ('rows', 'feat'), scatter_dimension=0, tiled=True)  1260 us
    psum x1, waiting for transfers between devices, local(): total_numer, total_counts = lax.psum((numer, counted), 'rows')  154 us
    psum x1, blocking collectives, local(): total_numer, total_counts = lax.psum((numer, counted), 'rows')  73.5 us
    all_gather x1, waiting for transfers between devices, local(): full_rotation = lax.all_gather(rotation, 'feat', axis=1, tiled=True)  58.8 us
  transfers between devices with their start and end apart: 5, of which 5 were waited for; matrix products, arithmetic and copies ran while one was open for 1% of the time, Pallas kernels for 0%

commit v1 on v0

v1 whole, which is shorter than its diff:
```python
import jax
import jax.numpy as jnp
from jax import lax
from jax.experimental import pallas as pl
from jax.experimental.pallas import tpu as pltpu
from jax.sharding import PartitionSpec as P

D = 1024
SUB = 64
K = 256
SW = D // SUB
W = 128
NS = W // SW
ROWS = 768
CHUNK = 256
HALF = D // 2 + K // 2 + NS
bf16 = jnp.bfloat16
f32 = jnp.float32


def dot(a, b, ca, cb):
    return lax.dot_general(a, b, (((ca,), (cb,)), ((), ())), preferred_element_type=f32)


def assign_kernel(data_ref, pack_ref, out_ref, xaug, reb, wb):
    codes_t = pack_ref[0, :, D:]
    codes = codes_t.astype(f32).T.astype(bf16)
    wide = codes.astype(f32)
    squares = wide * wide
    high = squares.astype(bf16)
    low = (squares - high.astype(f32)).astype(bf16)
    row_group = lax.broadcasted_iota(jnp.int32, (W, W), 0) // SW
    col_group = lax.broadcasted_iota(jnp.int32, (W, W), 1) // SW
    group_ones = jnp.where(row_group == col_group, 1.0, 0.0).astype(bf16)
    bias = -0.5 * (dot(high, group_ones, 1, 0) + dot(low, group_ones, 1, 0))
    lane = lax.broadcasted_iota(jnp.int32, (K, W), 1)
    b0 = bias.astype(bf16).astype(f32)
    b1 = (bias - b0).astype(bf16).astype(f32)
    b2 = bias - b0 - b1
    place = lane % SW
    aug = jnp.where(place == 0, b0, jnp.where(place == 1, b1, jnp.where(place == 2, b2, 0.0))).astype(bf16)
    xaug[0:W, :] = dot(pack_ref[0, :, :D], data_ref[...], 1, 0).astype(bf16)
    xaug[W:, :] = jnp.ones((W, ROWS), bf16)
    acc = jnp.zeros((K, 2 * W), f32)
    group2 = (lax.broadcasted_iota(jnp.int32, (K, 2 * W), 1) // SW) % NS
    zero = jnp.zeros((K, W), bf16)
    for s in range(NS):
        mask = (lane // SW) == s
        lhs = jnp.concatenate([jnp.where(mask, codes, zero), jnp.where(mask, aug, zero)], axis=1)
        for piece in range(ROWS // CHUNK):
            cols = slice(piece * CHUNK, (piece + 1) * CHUNK)
            logits = dot(lhs, xaug[:, cols], 1, 0)
            e = jnp.exp(logits - jnp.max(logits, axis=0, keepdims=True))
            wb[:, cols] = (e * (1.0 / jnp.sum(e, axis=0, keepdims=True))).astype(bf16)
        own = slice(s * SW, (s + 1) * SW)
        reb[own, :] = dot(pack_ref[0, own, D:], wb[...], 1, 0).astype(bf16)
        acc = jnp.where(group2 == s, dot(wb[...], xaug[...], 1, 1), acc)
    counts = acc[:, W:].T
    counts = jnp.concatenate([counts[s * SW : s * SW + 1] for s in range(NS)], axis=0)
    cross = dot(data_ref[...], reb[...], 1, 1)
    for h in range(2):
        out_ref[0, h, : D // 2, :] = cross[h * (D // 2) : (h + 1) * (D // 2)]
        out_ref[0, h, D // 2 : D // 2 + K // 2, :] = acc[h * (K // 2) : (h + 1) * (K // 2), :W]
        out_ref[0, h, D // 2 + K // 2 :, :] = counts[:, h * (K // 2) : (h + 1) * (K // 2)]


def assign(data_t, packs):
    blocks = packs.shape[0]
    return pl.pallas_call(
        assign_kernel,
        grid=(blocks,),
        in_specs=[
            pl.BlockSpec((D, ROWS), lambda g: (0, 0)),
            pl.BlockSpec((1, W, D + K), lambda g: (g, 0, 0)),
        ],
        out_specs=pl.BlockSpec((1, 2, HALF, W), lambda g: (g, 0, 0, 0)),
        out_shape=jax.ShapeDtypeStruct((blocks, 2, HALF, W), f32),
        scratch_shapes=[
            pltpu.VMEM((2 * W, ROWS), bf16),
            pltpu.VMEM((W, ROWS), bf16),
            pltpu.VMEM((K, ROWS), bf16),
        ],
        compiler_params=pltpu.CompilerParams(vmem_limit_bytes=48 * 1024 * 1024),
        name="assign",
    )(data_t, packs)


def local(data, rotation, codebook):
    n_feat = lax.axis_size("feat")
    n_rows = lax.axis_size("rows")
    pairs = n_rows // 2
    core = lax.axis_index("rows") % 2
    swap = [(i, i ^ 1) for i in range(n_rows)]
    lanes = D // n_rows
    data_t = data.reshape(ROWS, pairs, 2, lanes).transpose(2, 1, 3, 0).reshape(D, ROWS)
    rot_t = rotation.reshape(pairs, 2, lanes, W).transpose(3, 1, 0, 2).reshape(W, D)
    pack = jnp.concatenate([rot_t, codebook.T], axis=1)
    half = lax.dynamic_slice_in_dim(pack, core * (W // 2), W // 2, axis=0)
    mine = lax.all_to_all(
        jnp.broadcast_to(half[None], (n_feat,) + half.shape), "feat", split_axis=0, concat_axis=0, tiled=True
    )
    other = lax.ppermute(mine, "rows", swap)
    first = core == 0
    packs = jnp.concatenate([jnp.where(first, mine, other), jnp.where(first, other, mine)], axis=1)
    out = assign(data_t, packs)
    give = lax.dynamic_index_in_dim(out, 1 - core, axis=1, keepdims=False)
    keep = lax.dynamic_index_in_dim(out, core, axis=1, keepdims=False)
    summed = (keep + lax.ppermute(give, "rows", swap)).astype(LINK)
    got = lax.all_to_all(summed, "feat", split_axis=0, concat_axis=0, tiled=True)
    part = jnp.sum(got.astype(f32), axis=0)
    groups = [[i * 2 + c for i in range(pairs)] for c in range(2)]
    cross_part = part[: D // 2].reshape(pairs, lanes, W)
    numer_part = part[D // 2 : D // 2 + K // 2].reshape(pairs, K // n_rows, W)
    count_part = jnp.broadcast_to(part[D // 2 + K // 2 :][None], (pairs, NS, W))
    sent = jnp.concatenate([cross_part, numer_part, count_part], axis=1)
    total = jnp.sum(
        lax.all_to_all(sent, "rows", split_axis=0, concat_axis=0, tiled=True, axis_index_groups=groups), axis=0
    )
    cross = total[:lanes]
    tail = total[lanes:]
    whole = lax.all_to_all(
        jnp.broadcast_to(tail[None], (n_rows,) + tail.shape), "rows", split_axis=0, concat_axis=0, tiled=True
    )
    k_rows = K // n_rows
    numer = whole[:, :k_rows].reshape(pairs, 2, k_rows, W).transpose(1, 0, 2, 3).reshape(K, W)
    counts = whole[:2, k_rows:].transpose(1, 0, 2).reshape(NS, K)
    per_column = jnp.repeat(counts.T, SW, axis=1)
    new_codebook = (numer + codebook.astype(f32)) / (per_column + 1.0)
    return new_codebook, counts, cross


LINK = bf16


def solution(mesh):
    in_specs = (P(("rows", "feat"), None), P(None, "feat"), P(None, "feat"))
    out_specs = (P(None, "feat"), P("feat", None), P("rows", "feat"))
    return jax.shard_map(local, mesh=mesh, in_specs=in_specs, out_specs=out_specs, check_vma=False)
```

time: 1750 us -> 152 us (0.09)
  waiting for transfers between devices: 1510 us -> 19.1 us
  matrix products: 65.5 us -> 0 us
  Pallas kernels: 0 us -> 40.8 us
  local copies, waits for them, and re-layouts: 39.4 us -> 5.43 us
  other arithmetic: 26.3 us -> 7.4 us
    reduce_scatter x1 -> x0, waiting for transfers between devices: 1260 us -> none  [local(): lax.psum_scatter(ordered, ('rows', 'feat'), scatter_dimension=0, tiled=True)]
    psum x1 -> x0, waiting for transfers between devices: 154 us -> none  [local(): total_numer, total_counts = lax.psum((numer, counted), 'rows')]
    psum x1 -> x0, blocking collectives: 73.5 us -> none  [local(): total_numer, total_counts = lax.psum((numer, counted), 'rows')]
    all_to_all x0 -> x3, blocking collectives: none -> 69.3 us  [the longest x1 24.2 us: local(): lax.all_to_all(jnp.broadcast_to(half[None], (n_feat,) + half.shape), 'fea...]
    all_gather x1 -> x0, waiting for transfers between devices: 58.8 us -> none  [local(): full_rotation = lax.all_gather(rotation, 'feat', axis=1, tiled=True)]
    pallas_call x0 -> x1, Pallas kernels: none -> 40.8 us  [assign(): pl.pallas_call(assign_kernel, grid=(blocks,), in_specs=[pl.BlockSpec((D,...]
    sub x6 -> x0, matrix products: 32.8 us -> none  [step(): weights = jax.nn.softmax(logits, axis=-1)]
    dot_general x14 -> x0, matrix products: 32.7 us -> none  [the longest x6 17 us: step(): jnp.einsum('snk,ksd->nsd', weights_b, codes, preferred_element_type=jnp.f...]
  transfers between devices with their start and end apart: 5 -> 3, of which waited for: 5 -> 3; matrix products, arithmetic and copies ran while one was open for 1% -> 1% of each run, Pallas kernels for 0% -> 0%
where the time goes in v1:
time: 152 us; the launch traced here: 151 us
  blocking collectives  69.3 us (46%)
  Pallas kernels  40.8 us (27%)
  waiting for transfers between devices  19.1 us (13%)
  starting transfers between devices  8.28 us (5%)
  other arithmetic  7.4 us (5%)
  local copies, waits for them, and re-layouts  5.43 us (4%)
    pallas_call x1, Pallas kernels, assign(): pl.pallas_call(assign_kernel, grid=(blocks,), in_specs=[pl.BlockSpec((D,...  40.8 us
    all_to_all x1, blocking collectives, local(): lax.all_to_all(jnp.broadcast_to(half[None], (n_feat,) + half.shape), 'fea...  24.2 us
    all_to_all x1, blocking collectives, local(): lax.all_to_all(sent, 'rows', split_axis=0, concat_axis=0, tiled=True, axi...  24.1 us
    all_to_all x1, blocking collectives, local(): lax.all_to_all(summed, 'feat', split_axis=0, concat_axis=0, tiled=True)  21 us
    all_to_all x1, waiting for transfers between devices, local(): lax.all_to_all(jnp.broadcast_to(tail[None], (n_rows,) + tail.shape), 'row...  12.2 us
    all_to_all x1, starting transfers between devices, local(): lax.all_to_all(jnp.broadcast_to(tail[None], (n_rows,) + tail.shape), 'row...  5.96 us
    ppermute x1, waiting for transfers between devices, local(): summed = (keep + lax.ppermute(give, 'rows', swap)).astype(LINK)  4.71 us
  transfers between devices with their start and end apart: 3, of which 3 were waited for; matrix products, arithmetic and copies ran while one was open for 1% of the time, Pallas kernels for 0%

profile of v1, /device:TPU:1, one launch (start us, length us, event | category | flops | bytes accessed | tf_op | source)
XLA Modules:
  0.0 151.1 jit_solution(7831047714597885628)
XLA Ops:
  0.6 1.0 copy.24
  1.6 1.0 dynamic-slice_maximum_fusion
  2.6 0.2 copy.25
  2.8 0.1 broadcast_in_dim.8
  2.9 0.0 copy-start
  2.9 24.2 %all_to_all.20 = bf16[8,64,1280]{2,1,0:T(8,128)(2,1)} all-to-all(bf16[8,64,1280]{2,1,0:T(8,128)(2,1)S(1)} %broadcast_in_dim.8), channel_id=1, replica_groups=mesh['rows'=32,'feat'=8] {'feat'}, dimensions={0} | all-to-all | bytes 2621440 | tf_op jit(solution)/shard_map/all_to_all | solution.py:99
  27.1 1.9 %collective-permute-start = (bf16[8,64,1280]{2,1,0:T(8,128)(2,1)}, bf16[8,64,1280]{2,1,0:T(8,128)(2,1)}, u32[]{:S(2)}, u32[]{:S(2)}) collective-permute-start(bf16[8,64,1280]{2,1,0:T(8,128)(2,1)} %all_to_all.20), channel_id=1, source_target_pairs={{0,8},{8,0},{16,24},{24,16},{32,40},{40,32},{48,56},{56,48},{64,72... | collective-permute-start | bytes 3932168 | tf_op jit(solution)/shard_map/ppermute | solution.py:102
  28.9 0.0 copy-done
  28.9 0.7 copy.22
  29.7 0.1 copy.23
  29.8 2.2 %collective-permute-done = bf16[8,64,1280]{2,1,0:T(8,128)(2,1)} collective-permute-done((bf16[8,64,1280]{2,1,0:T(8,128)(2,1)}, bf16[8,64,1280]{2,1,0:T(8,128)(2,1)}, u32[]{:S(2)}, u32[]{:S(2)}) %collective-permute-start) | collective-permute-done | bytes 1310752 | tf_op jit(solution)/shard_map/ppermute | solution.py:102
  32.0 1.9 %broadcast_select_fusion.1 = (bf16[8,64,1280]{2,1,0:T(8,128)(2,1)S(1)}, bf16[8,64,1280]{2,1,0:T(8,128)(2,1)S(1)}) fusion(bf16[8,64,1280]{2,1,0:T(8,128)(2,1)} %all_to_all.20, bf16[8,64,1280]{2,1,0:T(8,128)(2,1)} %collective-permute-done, pred[]{:T(512)S(6)} %eq.5), kind=kLoop, calls=%fused_computation.6 | loop fusion | flops 1310720 | bytes 5242881 | tf_op jit(solution)/shard_map/jit(_where)/select_n | solution.py:104
  33.8 0.2 pad_maximum_fusion.pack_ref
  34.0 40.8 %assign.1 = f32[8,2,648,128]{3,2,1,0:T(8,128)} custom-call(bf16[1024,768]{1,0:T(8,128)(2,1)S(1)} %bitcast.33, bf16[8,128,1280]{2,1,0:T(8,128)(2,1)S(1)} %pad_maximum_fusion.pack_ref), custom_call_target="tpu_custom_call" | custom-call | tf_op jit(solution)/shard_map/assign/pallas_call | solution.py:69
  74.8 1.9 %dynamic-slice_bitcast_fusion = f32[8,648,128]{2,1,0:T(8,128)S(1)} fusion(f32[8,2,648,128]{3,2,1,0:T(8,128)} %assign.1, s32[]{:T(128)S(6)} %select_n.35), kind=kLoop, calls=%fused_computation.3 | loop fusion | bytes 5308420 | tf_op jit(solution)/shard_map/jit(dynamic_index_in_dim)/squeeze | solution.py:106
  76.7 0.5 collective-permute-start.1
  77.2 4.7 %collective-permute-done.1 = f32[8,648,128]{2,1,0:T(8,128)} collective-permute-done((f32[8,648,128]{2,1,0:T(8,128)S(1)}, f32[8,648,128]{2,1,0:T(8,128)}, u32[]{:S(2)}, u32[]{:S(2)}) %collective-permute-start.1) | collective-permute-done | bytes 2654240 | tf_op jit(solution)/shard_map/ppermute | solution.py:108
  81.9 2.8 %fusion = bf16[8,648,128]{2,1,0:T(8,128)(2,1)S(1)} fusion(f32[8,648,128]{2,1,0:T(8,128)} %collective-permute-done.1, f32[8,2,648,128]{3,2,1,0:T(8,128)} %assign.1, s32[]{:T(128)S(6)} %select_n.34), kind=kLoop, calls=%fused_computation.1 | loop fusion | flops 1327104 | bytes 6635524 | tf_op jit(solution)/shard_map/convert_element_type | solution.py:108
  84.7 21.0 %all_to_all.21 = bf16[8,648,128]{2,1,0:T(8,128)(2,1)S(1)} all-to-all(bf16[8,648,128]{2,1,0:T(8,128)(2,1)S(1)} %fusion), channel_id=1, replica_groups=mesh['rows'=32,'feat'=8] {'feat'}, dimensions={0} | all-to-all | bytes 2654208 | tf_op jit(solution)/shard_map/all_to_all | solution.py:109
  105.7 0.2 convert_reduce_fusion
  106.0 0.0 copy-start.1
  106.0 24.1 %all_to_all.22 = f32[16,48,128]{2,1,0:T(8,128)S(1)} all-to-all(f32[16,48,128]{2,1,0:T(8,128)S(1)} %pad_maximum_fusion.1), channel_id=1, replica_groups={{0,16,32,48,64,80,96,112,128,144,160,176,192,208,224,240},{8,24,40,56,7..., dimensions={0} | all-to-all | bytes 786432 | tf_op jit(solution)/shard_map/all_to_all | solution.py:117
  130.2 0.7 broadcast_in_dim.10
  130.9 6.0 %all-to-all-start.3 = ((f32[32,16,128]{2,1,0:T(8,128)}), f32[32,16,128]{2,1,0:T(8,128)S(1)}, u32[]{:S(2)}, u32[]{:S(2)}) async-start(f32[32,16,128]{2,1,0:T(8,128)} %broadcast_in_dim.10), calls=%async_computation.3 | async-start | bytes 524288 | tf_op jit(solution)/shard_map/all_to_all | solution.py:121
  136.8 0.6 slice.34
  137.4 12.2 %all-to-all-done.3 = f32[32,16,128]{2,1,0:T(8,128)S(1)} async-done(((f32[32,16,128]{2,1,0:T(8,128)}), f32[32,16,128]{2,1,0:T(8,128)S(1)}, u32[]{:S(2)}, u32[]{:S(2)}) %all-to-all-start.3) | async-done | bytes 262176 | tf_op jit(solution)/shard_map/all_to_all | solution.py:121
  149.7 0.6 add_bitcast_fusion
  150.3 0.1 copy.27
  150.4 0.0 copy-done.1
  150.4 0.7 fusion.1
  (10 shorter events, 0.1 us)
Async XLA Ops:
  2.9 26.1 %copy-start = (bf16[768,1024]{1,0:T(8,128)(2,1)S(1)}, bf16[768,1024]{1,0:T(8,128)(2,1)}, u32[]{:S(2)}) copy-start(bf16[768,1024]{1,0:T(8,128)(2,1)} %param.3) | copy-start | bytes 4718596
  27.1 4.9 %collective-permute-start = (bf16[8,64,1280]{2,1,0:T(8,128)(2,1)}, bf16[8,64,1280]{2,1,0:T(8,128)(2,1)}, u32[]{:S(2)}, u32[]{:S(2)}) collective-permute-start(bf16[8,64,1280]{2,1,0:T(8,128)(2,1)} %all_to_all.20), channel_id=1, source_target_pairs={{0,8},{8,0},{16,24},{24,16},{32,40},{40,32},{48,56},{56,48},{64,72... | collective-permute-start | bytes 3932168 | tf_op jit(solution)/shard_map/ppermute | solution.py:102
  76.7 5.2 %collective-permute-start.1 = (f32[8,648,128]{2,1,0:T(8,128)S(1)}, f32[8,648,128]{2,1,0:T(8,128)}, u32[]{:S(2)}, u32[]{:S(2)}) collective-permute-start(f32[8,648,128]{2,1,0:T(8,128)S(1)} %dynamic-slice_bitcast_fusion), channel_id=1, source_target_pairs={{0,8},{8,0},{16,24},{24,16},{32,40},{40,32},{48,56},{56,48},{64,72... | collective-permute-start | bytes 7962632 | tf_op jit(solution)/shard_map/ppermute | solution.py:108
  106.0 44.4 %copy-start.1 = (bf16[256,128]{1,0:T(8,128)(2,1)S(1)}, bf16[256,128]{1,0:T(8,128)(2,1)}, u32[]{:S(2)}) copy-start(bf16[256,128]{1,0:T(8,128)(2,1)} %param.5) | copy-start | bytes 196612
  130.9 18.8 %all-to-all-start.3 = ((f32[32,16,128]{2,1,0:T(8,128)}), f32[32,16,128]{2,1,0:T(8,128)S(1)}, u32[]{:S(2)}, u32[]{:S(2)}) async-start(f32[32,16,128]{2,1,0:T(8,128)} %broadcast_in_dim.10), calls=%async_computation.3 | async-start | bytes 524288 | tf_op jit(solution)/shard_map/all_to_all | solution.py:121
